TPU v7x, 512 devices: a whole 4x4x16 slice. The times are simulated.
512 devices in a mesh: section: 2 (over x_hi), gy: 16 (over y, x_lo, core), gx: 16 (over z).
Axes of the slice: x: 4 (x_hi: 2, x_lo: 2; x = x_hi * 2 + x_lo), y: 4, z: 16, core: 2. Of those that a mesh axis runs over, the one named last changes fastest.
Arguments:
- images: bfloat16 [2, 512, 1024, 128], P('section', 'gy', 'gx'), may hold values from -6 to 6
- first_kernel: bfloat16 [3, 3, 128, 128], replicated, may hold values from -0.1875 to 0.1875
- projection: bfloat16 [128, 256], replicated, may hold values from -0.5 to 0.5
- second_kernel: bfloat16 [3, 3, 256, 256], replicated, may hold values from -0.125 to 0.125
- cotangent: bfloat16 [2, 256, 512, 256], P('section', 'gy', 'gx'), may hold values from -0.15625 to 0.15625
Outputs:
- features: bfloat16 [2, 256, 512, 256], P('section', 'gy', 'gx')
- grad_first: float32 [3, 3, 128, 128], replicated
- grad_projection: float32 [128, 256], replicated
- grad_second: float32 [3, 3, 256, 256], replicated
All inputs are finite; a program needn't handle non-finite values.
Results may differ from a plain program's by a relative error of at most 0.014.
Values may be sent and summed in bfloat16 or wider, within the bound.
A program may use at most 64 MiB of HBM per device.

v0:
```python
import jax
import jax.numpy as jnp
from jax import lax
from jax.sharding import PartitionSpec as P


def padded_2(array, sides, width):
    for axis, dim in sides:
        size, length = (lax.axis_size(axis), array.shape[dim])
        up = [(i, (i + 1) % size) for i in range(size - 1)]
        down = [(j, i) for i, j in up]
        last = lax.slice_in_dim(array, length - width, length, axis=dim)
        initial = lax.slice_in_dim(array, 0, width, axis=dim)
        before = lax.ppermute(last, axis, up)
        after = lax.ppermute(initial, axis, down)
        array = jnp.concatenate([before, array, after], axis=dim)
    return array


def from_partner(block, axis, bit):
    count = lax.axis_size(axis)
    route = []
    for low in range(count):
        high = low | 1 << bit
        if high != low and high < count:
            route += [(low, high), (high, low)]
    return lax.ppermute(block, axis, route)


def silu_slope(values):
    sigma = jax.nn.sigmoid(values)
    return sigma * (1.0 + values * (1.0 - sigma))


def conv_forward(padded, kernel, row_count, col_count):
    total = jnp.zeros((row_count * col_count, kernel.shape[3]), jnp.float32)
    for row_tap in range(3):
        for col_tap in range(3):
            piece = padded[row_tap : row_tap + row_count, col_tap : col_tap + col_count].reshape(
                row_count * col_count, padded.shape[2]
            )
            total = total + jnp.dot(
                piece, kernel[row_tap, col_tap], preferred_element_type=jnp.float32
            )
    return total


def conv_slopes(padded, slope, row_count, col_count):
    pieces = []
    for row_tap in range(3):
        for col_tap in range(3):
            piece = padded[row_tap : row_tap + row_count, col_tap : col_tap + col_count].reshape(
                row_count * col_count, padded.shape[2]
            )
            pieces.append(jnp.einsum("pc,pd->cd", piece, slope, preferred_element_type=jnp.float32))
    return jnp.stack(pieces).reshape(3, 3, padded.shape[2], slope.shape[1])


def conv_back(padded, kernel, row_count, col_count):
    total = jnp.zeros((row_count * col_count, kernel.shape[2]), jnp.float32)
    for row_tap in range(3):
        for col_tap in range(3):
            piece = padded[
                2 - row_tap : 2 - row_tap + row_count, 2 - col_tap : 2 - col_tap + col_count
            ].reshape(row_count * col_count, padded.shape[2])
            total = total + jnp.einsum(
                "pd,cd->pc", piece, kernel[row_tap, col_tap], preferred_element_type=jnp.float32
            )
    return total


def first_forward(tile, first_kernel):
    row_count, col_count, channels = tile.shape
    padded = padded_2(tile, (("gy", 0), ("gx", 1)), 1)
    before = conv_forward(padded, first_kernel, row_count, col_count)
    hidden = jax.nn.silu(before).astype(jnp.bfloat16).reshape(row_count, col_count, channels)
    pooled = (
        hidden.astype(jnp.float32)
        .reshape(row_count // 2, 2, col_count // 2, 2, channels)
        .sum(axis=(1, 3))
        * 0.25
    ).astype(jnp.bfloat16)
    return (padded, before, pooled)


def project(pooled, projection):
    half_rows, half_cols, channels = pooled.shape
    flat = jnp.dot(
        pooled.reshape(half_rows * half_cols, channels),
        projection,
        preferred_element_type=jnp.float32,
    )
    return flat.astype(jnp.bfloat16).reshape(half_rows, half_cols, projection.shape[1])


def second_pass(middle, second_kernel, upstream):
    half_rows, half_cols, wide = middle.shape
    padded = padded_2(middle, (("gy", 0), ("gx", 1)), 1)
    before = conv_forward(padded, second_kernel, half_rows, half_cols)
    output = jax.nn.silu(before).astype(jnp.bfloat16).reshape(half_rows, half_cols, wide)
    flat_up = upstream.reshape(half_rows * half_cols, wide).astype(jnp.float32)
    slope = (flat_up * silu_slope(before)).astype(jnp.bfloat16)
    kernel_grad = conv_slopes(padded, slope, half_rows, half_cols)
    slope_padded = padded_2(slope.reshape(half_rows, half_cols, wide), (("gy", 0), ("gx", 1)), 1)
    back = conv_back(slope_padded, second_kernel, half_rows, half_cols).astype(jnp.bfloat16)
    return (output, kernel_grad, back.reshape(half_rows, half_cols, wide))


def projection_back(pooled, back, projection):
    half_rows, half_cols, channels = pooled.shape
    flat_pool = pooled.reshape(half_rows * half_cols, channels)
    flat_back = back.reshape(half_rows * half_cols, back.shape[2])
    grad = jnp.einsum("pc,pd->cd", flat_pool, flat_back, preferred_element_type=jnp.float32)
    pooled_slope = jnp.einsum(
        "pd,cd->pc", flat_back, projection, preferred_element_type=jnp.float32
    )
    return (grad, pooled_slope.astype(jnp.bfloat16).reshape(half_rows, half_cols, channels))


def first_back(padded, before, pooled_slope):
    half_rows, half_cols, channels = pooled_slope.shape
    spread = jnp.broadcast_to(
        (pooled_slope.astype(jnp.float32) * 0.25)[:, None, :, None, :],
        (half_rows, 2, half_cols, 2, channels),
    )
    spread = spread.reshape(4 * half_rows * half_cols, channels)
    slope = (spread * silu_slope(before)).astype(jnp.bfloat16)
    return conv_slopes(padded, slope, 2 * half_rows, 2 * half_cols)


def per_device(images, first_kernel, projection, second_kernel, cotangent):
    padded, before, pooled = first_forward(images[0], first_kernel)
    middle = from_partner(project(pooled, projection), "section", 0)
    output, grad_second, back_far = second_pass(middle, second_kernel, cotangent[0])
    back = from_partner(back_far, "section", 0)
    grad_projection, pooled_slope = projection_back(pooled, back, projection)
    grad_first = first_back(padded, before, pooled_slope)
    grad_first, grad_projection, grad_second = lax.psum(
        (grad_first, grad_projection, grad_second), ("section", "gy", "gx")
    )
    return (output[None], grad_first, grad_projection, grad_second)


def solution(mesh):
    placed = (P("section", "gy", "gx", None), P(), P(), P(), P("section", "gy", "gx", None))
    return jax.shard_map(
        per_device,
        mesh=mesh,
        in_specs=placed,
        out_specs=(P("section", "gy", "gx", None), P(), P(), P()),
        check_vma=False,
    )
```

profile of v0, /device:TPU:2, one launch (start us, length us, event | category | flops | bytes accessed | tf_op | source)
XLA Modules:
  0.0 605.1 jit_solution(15916452577856336045)
XLA Ops:
  7.2 0.8 slice_bitcast_fusion.3
  8.0 1.9 collective-permute-start
  10.0 3.6 collective-permute-start.1
  13.6 1.4 collective-permute-done.1
  15.0 0.9 pad_maximum_fusion.15
  15.9 3.8 collective-permute-start.2
  19.8 1.4 collective-permute-start.3
  21.2 1.3 pad_maximum_fusion.1
  22.8 2.7 collective-permute-done.3
  29.0 0.9 convert_reduce_fusion
  30.1 4.1 collective-permute-start.4
  34.3 8.2 %collective-permute-done.4 = bf16[16,32,256]{2,1,0:T(8,128)(2,1)S(1)} collective-permute-done((bf16[16,32,256]{2,1,0:T(8,128)(2,1)S(1)}, bf16[16,32,256]{2,1,0:T(8,128)(2,1)S(1)}, u32[]{:S(2)}, u32[]{:S(2)}) %collective-permute-start.4) | collective-permute-done | bytes 262176 | tf_op jit(solution)/shard_map/ppermute | solution.py:27
  42.5 2.1 collective-permute-start.5
  44.6 3.5 collective-permute-start.6
  48.1 1.4 collective-permute-done.6
  49.6 3.8 collective-permute-start.7
  53.5 1.3 collective-permute-start.8
  55.3 4.9 collective-permute-done.8
  61.9 0.7 copy-done.7
  62.6 1.1 fusion.26
  64.1 3.1 collective-permute-start.9
  67.2 2.5 collective-permute-start.10
  71.4 1.3 collective-permute-start.11
  72.7 6.0 collective-permute-start.12
  79.0 1.1 collective-permute-done.12
  82.7 4.0 collective-permute-start.13
  87.2 7.4 %collective-permute-done.13 = bf16[16,32,256]{2,1,0:T(8,128)(2,1)S(1)} collective-permute-done((bf16[16,32,256]{2,1,0:T(8,128)(2,1)S(1)}, bf16[16,32,256]{2,1,0:T(8,128)(2,1)S(1)}, u32[]{:S(2)}, u32[]{:S(2)}) %collective-permute-start.13) | collective-permute-done | bytes 262176 | tf_op jit(solution)/shard_map/ppermute | solution.py:27
  99.0 0.9 convolution_bitcast_fusion.9
  99.9 492.5 %all-reduce.3.cloned.1.call-done = (f32[3,3,128,128]{3,2,1,0:T(8,128)}, f32[128,256]{1,0:T(8,128)}, f32[3,3,256,256]{3,2,1,0:T(8,128)}) async-done(((f32[3,3,128,128]{3,2,1,0:T(8,128)}, f32[128,256]{1,0:T(8,128)}, f32[3,3,256,256]{3,2,1,0:T(8,128)}), (f32[3,3,128,128]{3,2,1,0:T(8,128)}, f32[128,256]{1,0:T(8,128)}, f32[3,3,256,256]{3,2,1,0:T(8,128)})) %all-reduce.3.cloned.1.call-update) | async-done | bytes 3080208 | tf_op jit(solution)/shard_map/psum | solution.py:138
  592.4 2.0 copy.32
  594.4 0.7 copy.33
  595.0 3.2 copy.34
  (87 shorter events, 15.9 us)
Async XLA Ops:
  7.2 22.7 %copy-start = (bf16[128,256]{1,0:T(8,128)(2,1)S(1)}, bf16[128,256]{1,0:T(8,128)(2,1)}, u32[]{:S(2)}) copy-start(bf16[128,256]{1,0:T(8,128)(2,1)} %param.7) | copy-start | bytes 196612
  7.2 15.3 %copy-start.5 = (bf16[3,3,128,128]{3,2,1,0:T(8,128)(2,1)S(1)}, bf16[3,3,128,128]{3,2,1,0:T(8,128)(2,1)}, u32[]{:S(2)}) copy-start(bf16[3,3,128,128]{3,2,1,0:T(8,128)(2,1)} %param.6) | copy-start | bytes 884740
  7.2 585.2 %all-reduce.3.cloned.1.call-start = ((), (), s32[]{:S(2)}) async-start(), calls=%async_computation | async-start | bytes 6160384 | tf_op jit(solution)/shard_map/psum | solution.py:138
  8.0 5.6 collective-permute-start
  10.0 5.1 collective-permute-start.1
  15.9 6.9 %collective-permute-start.2 = (bf16[34,1,128]{2,1,0:T(2,128)(2,1)S(1)}, bf16[34,1,128]{2,1,0:T(2,128)(2,1)S(1)}, u32[]{:S(2)}, u32[]{:S(2)}) collective-permute-start(bf16[34,1,128]{2,1,0:T(2,128)(2,1)S(1)} %get-tuple-element.15), channel_id=1, source_target_pairs={{0,1},{1,2},{2,3},{3,4},{4,5},{5,6},{6,7},{7,8},{8,9},{9,10},{10,1... | collective-permute-start | bytes 26120 | tf_op jit(solution)/shard_map/ppermute | solution.py:14
  19.8 5.8 copy-start.1
  19.8 5.8 collective-permute-start.3
  29.9 24.9 %copy-start.2 = (bf16[3,3,256,256]{3,2,1,0:T(8,128)(2,1)S(1)}, bf16[3,3,256,256]{3,2,1,0:T(8,128)(2,1)}, u32[]{:S(2)}) copy-start(bf16[3,3,256,256]{3,2,1,0:T(8,128)(2,1)} %param.8) | copy-start | bytes 3538948
  30.1 12.4 %collective-permute-start.4 = (bf16[16,32,256]{2,1,0:T(8,128)(2,1)S(1)}, bf16[16,32,256]{2,1,0:T(8,128)(2,1)S(1)}, u32[]{:S(2)}, u32[]{:S(2)}) collective-permute-start(bf16[16,32,256]{2,1,0:T(8,128)(2,1)S(1)} %bitcast.328), channel_id=1, source_target_pairs={{0,256},{256,0},{1,257},{257,1},{2,258},{258,2},{3,259},{259,3},{4... | collective-permute-start | bytes 786440 | tf_op jit(solution)/shard_map/ppermute | solution.py:27
  42.5 5.6 collective-permute-start.5
  44.6 4.9 collective-permute-start.6
  49.6 5.6 collective-permute-start.7
  53.5 6.7 %collective-permute-start.8 = (bf16[18,1,256]{2,1,0:T(2,128)(2,1)S(1)}, bf16[18,1,256]{2,1,0:T(2,128)(2,1)S(1)}, u32[]{:S(2)}, u32[]{:S(2)}) collective-permute-start(bf16[18,1,256]{2,1,0:T(2,128)(2,1)S(1)} %get-tuple-element.43), channel_id=1, source_target_pairs={{1,0},{2,1},{3,2},{4,3},{5,4},{6,5},{7,6},{8,7},{9,8},{10,9},{11,1... | collective-permute-start | bytes 27656 | tf_op jit(solution)/shard_map/ppermute | solution.py:15
  61.7 1.0 copy-start.7
  64.1 7.3 %collective-permute-start.9 = (bf16[1,32,256]{2,1,0:T(8,128)(2,1)S(1)}, bf16[1,32,256]{2,1,0:T(8,128)(2,1)S(1)}, u32[]{:S(2)}, u32[]{:S(2)}) collective-permute-start(bf16[1,32,256]{2,1,0:T(8,128)(2,1)S(1)} %get-tuple-element.46), channel_id=1, source_target_pairs={{0,16},{16,32},{32,48},{48,64},{64,80},{80,96},{96,112},{112,128},... | collective-permute-start | bytes 49160 | tf_op jit(solution)/shard_map/ppermute | solution.py:14
  67.2 4.2 collective-permute-start.10
  71.4 7.6 %collective-permute-start.11 = (bf16[18,1,256]{2,1,0:T(2,128)(2,1)S(1)}, bf16[18,1,256]{2,1,0:T(2,128)(2,1)S(1)}, u32[]{:S(2)}, u32[]{:S(2)}) collective-permute-start(bf16[18,1,256]{2,1,0:T(2,128)(2,1)S(1)} %get-tuple-element.37), channel_id=1, source_target_pairs={{1,0},{2,1},{3,2},{4,3},{5,4},{6,5},{7,6},{8,7},{9,8},{10,9},{11,1... | collective-permute-start | bytes 27656 | tf_op jit(solution)/shard_map/ppermute | solution.py:15
  72.7 7.4 %collective-permute-start.12 = (bf16[18,1,256]{2,1,0:T(2,128)(2,1)S(1)}, bf16[18,1,256]{2,1,0:T(2,128)(2,1)S(1)}, u32[]{:S(2)}, u32[]{:S(2)}) collective-permute-start(bf16[18,1,256]{2,1,0:T(2,128)(2,1)S(1)} %get-tuple-element.38), channel_id=1, source_target_pairs={{0,1},{1,2},{2,3},{3,4},{4,5},{5,6},{6,7},{7,8},{8,9},{9,10},{10,1... | collective-permute-start | bytes 27656 | tf_op jit(solution)/shard_map/ppermute | solution.py:14
  82.7 12.0 %collective-permute-start.13 = (bf16[16,32,256]{2,1,0:T(8,128)(2,1)S(1)}, bf16[16,32,256]{2,1,0:T(8,128)(2,1)S(1)}, u32[]{:S(2)}, u32[]{:S(2)}) collective-permute-start(bf16[16,32,256]{2,1,0:T(8,128)(2,1)S(1)} %bitcast.329), channel_id=1, source_target_pairs={{0,256},{256,0},{1,257},{257,1},{2,258},{258,2},{3,259},{259,3},{4... | collective-permute-start | bytes 786440 | tf_op jit(solution)/shard_map/ppermute | solution.py:27
  87.2 8.6 %copy-start.3 = (f32[9,256,256]{2,1,0:T(8,128)}, f32[9,256,256]{2,1,0:T(8,128)S(1)}, u32[]{:S(2)}) copy-start(f32[9,256,256]{2,1,0:T(8,128)S(1)} %fusion.6) | copy-start | bytes 7077892
  99.0 0.9 copy-start.4
  592.4 2.0 copy-start.6
Sparse Core Ops, SparseCore 0:
  100.1 492.3 all-reduce.2
where the time goes:
time: 606 us; the launch traced here: 605 us
  waiting for transfers between devices  520 us (86%)
  starting transfers between devices  42.4 us (7%)
  matrix products  14.9 us (2%)
  between operations  14.7 us (2%)
  local copies, waits for them, and re-layouts  8.72 us (1%)
    psum x1, waiting for transfers between devices, per_device(): lax.psum((grad_first, grad_projection, grad_second), ('section', 'gy', 'g...  492 us
    ppermute x6, starting transfers between devices, padded_2(): before = lax.ppermute(last, axis, up)  20.7 us
    ppermute x2, waiting for transfers between devices, from_partner(): return lax.ppermute(block, axis, route)  15.7 us
    ppermute x6, starting transfers between devices, padded_2(): after = lax.ppermute(initial, axis, down)  13.6 us
  transfers between devices with their start and end apart: 15, of which 8 were waited for; matrix products, arithmetic and copies ran while one was open for 1% of the time, Pallas kernels for 0%

commit v1 on v0

--- a/solution.py
+++ b/solution.py
@@ -1,7 +1,15 @@
+import functools
 import jax
 import jax.numpy as jnp
 from jax import lax
 from jax.sharding import PartitionSpec as P
+
+
+def streams_arrange(original, row_axis, axis_key):
+    return lax.psum(lax.psum(original, row_axis), axis_key)
+
+
+ticks_solve = functools.partial(streams_arrange, row_axis=("gy", "gx"), axis_key="section")
 
 
 def padded_2(array, sides, width):
@@ -135,8 +143,8 @@
     back = from_partner(back_far, "section", 0)
     grad_projection, pooled_slope = projection_back(pooled, back, projection)
     grad_first = first_back(padded, before, pooled_slope)
-    grad_first, grad_projection, grad_second = lax.psum(
-        (grad_first, grad_projection, grad_second), ("section", "gy", "gx")
+    grad_first, grad_projection, grad_second = ticks_solve(
+        (grad_first, grad_projection, grad_second)
     )
     return (output[None], grad_first, grad_projection, grad_second)
 

time: 606 us -> 2310 us (3.81)
  the two profiles are of different devices: /device:TPU:2 before, /device:TPU:1 now
where the time goes in v1:
time: 2310 us
  waiting for transfers between devices  2220 us (96%)
  starting transfers between devices  45.8 us (2%)
    psum x2, waiting for transfers between devices, streams_arrange(): return lax.psum(lax.psum(original, row_axis), axis_key)  2190 us
  transfers between devices with their start and end apart: 16, of which 10 were waited for; matrix products, arithmetic and copies ran while one was open for 0% of the time, Pallas kernels for 0%

profile of v1, /device:TPU:1, one launch (start us, length us, event | category | flops | bytes accessed | tf_op | source)
XLA Modules:
  0.0 2305.6 jit_solution(9248893497096286253)
XLA Ops:
  7.2 0.8 slice_bitcast_fusion.3
  8.0 4.5 collective-permute-start
  12.5 5.6 collective-permute-start.1
  18.1 0.8 collective-permute-done.1
  18.9 0.9 pad_maximum_fusion.15
  19.8 2.2 collective-permute-start.2
  22.1 1.4 collective-permute-start.3
  23.5 1.3 pad_maximum_fusion.1
  25.1 1.8 collective-permute-done.3
  30.3 0.9 convert_reduce_fusion
  31.5 4.5 collective-permute-start.4
  36.0 6.5 collective-permute-done.4
  42.5 4.5 collective-permute-start.5
  47.0 1.9 collective-permute-start.6
  49.0 3.1 collective-permute-done.6
  52.2 3.6 collective-permute-start.7
  55.8 1.3 collective-permute-start.8
  57.6 4.0 collective-permute-done.8
  63.4 0.7 copy-done.7
  64.1 1.1 fusion.26
  65.5 3.1 collective-permute-start.9
  68.6 1.9 collective-permute-start.10
  72.2 1.4 collective-permute-done.10
  73.7 1.3 collective-permute-start.11
  75.0 5.7 collective-permute-start.12
  84.1 4.3 collective-permute-start.13
  89.0 5.9 collective-permute-done.13
  99.3 0.9 convolution_bitcast_fusion.9
  100.3 2085.0 %all-reduce.5.cloned.1.call-done = (f32[3,3,128,128]{3,2,1,0:T(8,128)}, f32[128,256]{1,0:T(8,128)}, f32[3,3,256,256]{3,2,1,0:T(8,128)}) async-done(((f32[3,3,128,128]{3,2,1,0:T(8,128)}, f32[128,256]{1,0:T(8,128)}, f32[3,3,256,256]{3,2,1,0:T(8,128)}), (f32[3,3,128,128]{3,2,1,0:T(8,128)}, f32[128,256]{1,0:T(8,128)}, f32[3,3,256,256]{3,2,1,0:T(8,128)})) %all-reduce.5.cloned.1.call-update) | async-done | bytes 3080208 | tf_op jit(solution)/shard_map/psum | solution.py:9
  2185.3 107.7 %all-reduce.7.cloned.1.call-done = (f32[3,3,128,128]{3,2,1,0:T(8,128)}, f32[128,256]{1,0:T(8,128)}, f32[3,3,256,256]{3,2,1,0:T(8,128)}) async-done(((f32[3,3,128,128]{3,2,1,0:T(8,128)}, f32[128,256]{1,0:T(8,128)}, f32[3,3,256,256]{3,2,1,0:T(8,128)}), (f32[3,3,128,128]{3,2,1,0:T(8,128)}, f32[128,256]{1,0:T(8,128)}, f32[3,3,256,256]{3,2,1,0:T(8,128)})) %all-reduce.7.cloned.1.call-update) | async-done | bytes 3080208 | tf_op jit(solution)/shard_map/psum | solution.py:9
  2293.0 2.0 copy.35
  2295.6 3.2 copy.37
  (90 shorter events, 17.1 us)
Async XLA Ops:
  7.2 24.1 %copy-start = (bf16[128,256]{1,0:T(8,128)(2,1)S(1)}, bf16[128,256]{1,0:T(8,128)(2,1)}, u32[]{:S(2)}) copy-start(bf16[128,256]{1,0:T(8,128)(2,1)} %param.7) | copy-start | bytes 196612
  7.2 17.6 copy-start.5
  7.2 2178.1 %all-reduce.5.cloned.1.call-start = ((), (), s32[]{:S(2)}) async-start(), calls=%async_computation | async-start | bytes 6160384 | tf_op jit(solution)/shard_map/psum | solution.py:9
  8.0 10.1 collective-permute-start
  12.5 6.4 collective-permute-start.1
  19.8 5.3 collective-permute-start.2
  22.1 4.8 copy-start.1
  22.1 4.8 collective-permute-start.3
  31.2 25.9 %copy-start.2 = (bf16[3,3,256,256]{3,2,1,0:T(8,128)(2,1)S(1)}, bf16[3,3,256,256]{3,2,1,0:T(8,128)(2,1)}, u32[]{:S(2)}) copy-start(bf16[3,3,256,256]{3,2,1,0:T(8,128)(2,1)} %param.8) | copy-start | bytes 3538948
  31.5 11.0 collective-permute-start.4
  42.5 6.5 collective-permute-start.5
  47.0 5.1 collective-permute-start.6
  52.2 5.3 collective-permute-start.7
  55.8 5.8 collective-permute-start.8
  63.1 1.0 copy-start.7
  65.5 6.7 collective-permute-start.9
  68.6 5.1 collective-permute-start.10
  73.7 7.3 collective-permute-start.11
  75.0 6.6 collective-permute-start.12
  84.1 10.8 collective-permute-start.13
  89.0 7.1 copy-start.3
  99.3 0.9 copy-start.4
  100.2 2192.7 %all-reduce.7.cloned.1.call-start = ((), (), s32[]{:S(2)}) async-start(), calls=%async_computation.1 | async-start | bytes 6160384 | tf_op jit(solution)/shard_map/psum | solution.py:9
  2293.0 2.0 copy-start.6
Sparse Core Ops, SparseCore 0:
  100.3 2084.8 all-reduce.4
  2188.6 104.2 all-reduce.6
